TPU v7x, 128 devices: a whole 4x4x4 slice. The times are simulated.
128 devices in a mesh: node: 8 (over z, y_lo), local: 16 (over x, y_hi, core).
Axes of the slice: x: 4, y: 4 (y_hi: 2, y_lo: 2; y = y_hi * 2 + y_lo), z: 4, core: 2. Of those that a mesh axis runs over, the one named last changes fastest.
Arguments:
- tokens: bfloat16 [16384, 2048], P(('node', 'local')), may hold values from -24 to 24
- expert_ids: int32 [16384, 2], P(('node', 'local')), may hold values from 0 to 127, as said below
- gate_code: int32 [16384], P(('node', 'local')), may hold values from 1 to 7
- grad_out: bfloat16 [16384, 2048], P(('node', 'local')), may hold values from -3 to 3
- up_weight: bfloat16 [128, 2048, 1024], P(('node', 'local')), may hold values from -0.125 to 0.125
- down_weight: bfloat16 [128, 1024, 2048], P(('node', 'local')), may hold values from -0.1875 to 0.1875
- shared_up: bfloat16 [2048, 1024], P('local'), may hold values from -0.125 to 0.125
- shared_down: bfloat16 [1024, 2048], P('local'), may hold values from -0.1875 to 0.1875
Outputs:
- layer_out: bfloat16 [16384, 2048], P(('node', 'local'))
- grad_tokens: bfloat16 [16384, 2048], P(('node', 'local'))
- grad_up: bfloat16 [128, 2048, 1024], P(('node', 'local'))
- grad_down: bfloat16 [128, 1024, 2048], P(('node', 'local'))
- grad_shared_up: float32 [2048, 1024], P('local')
- grad_shared_down: float32 [1024, 2048], P('local')
Inputs may be any that keep to these rules, and one draw needn't show every extreme that they name: `expert_ids`: each token names two different experts. In each block of 128 consecutive tokens no expert is named by more than 4 tokens, and one expert, the same in every block, is named by exactly 4 tokens of every block.
All inputs are finite; a program needn't handle non-finite values.
Results may differ from a plain program's by a relative error of at most 0.0058.
Values may be sent and summed in bfloat16 or wider, within the bound.
No kernel may reach another device: no remote copies, remote signals or barrier semaphores. Data moves between devices by JAX's collectives and lax.ppermute only.
A program may use at most 128 MiB of HBM per device.

v0:
```python
import jax
import jax.numpy as jnp
from jax import lax
from jax.sharding import Mesh, PartitionSpec as P

half_root = 0.7071067811865476
inv_root_tau = 0.3989422804014327

AXES = ("z", "ylo", "x", "yhi", "core")
CHIPS = ("z", "ylo", "x", "yhi")
LOCAL = ("x", "yhi")
NODE = ("z", "ylo")


def gelu_value(values):
    return 0.5 * values * (1.0 + lax.erf(values * half_root))


def gelu_slope(values):
    return 0.5 * (1.0 + lax.erf(values * half_root)) + values * inv_root_tau * jnp.exp(
        -0.5 * values * values
    )


def dot(left, right):
    return jnp.dot(left, right, preferred_element_type=jnp.float32)


def contract_rows(left, right):
    return lax.dot_general(
        left, right, (((0,), (0,)), ((), ())), preferred_element_type=jnp.float32
    )


def contract_cols(left, right):
    return lax.dot_general(
        left, right, (((1,), (1,)), ((), ())), preferred_element_type=jnp.float32
    )


def together(*arrays):
    return lax.optimization_barrier(arrays)


def swap(values):
    return lax.ppermute(values, "core", [(0, 1), (1, 0)])


def exchange(values):
    return lax.all_to_all(values, CHIPS, split_axis=0, concat_axis=0, tiled=True)


def body(tokens, expert_ids, gate_code, grad_out, up_weight, down_weight, shared_up, shared_down):
    core = lax.axis_index("core")
    rows, width = tokens.shape
    chips = lax.axis_size("z") * lax.axis_size("ylo") * lax.axis_size("x") * lax.axis_size("yhi")
    cap = 4 * rows // (2 * chips)
    slots = chips * 2 * cap

    chip_tokens = jnp.concatenate([tokens, swap(tokens)], axis=0)
    chip_grads = jnp.concatenate([grad_out, swap(grad_out)], axis=0)

    id_rows = expert_ids.T
    order = jnp.arange(rows, dtype=jnp.int32)
    earlier = order[:, None] < order[None, :]
    positions = []
    for column in range(2):
        same = (expert_ids[:, 0:1] == id_rows[column : column + 1]) | (
            expert_ids[:, 1:2] == id_rows[column : column + 1]
        )
        positions.append(jnp.sum((same & earlier).astype(jnp.int32), axis=0))
    routes = jnp.stack(
        [id_rows[0] * cap + positions[0], id_rows[1] * cap + positions[1], gate_code]
    )
    routes_other = swap(routes)

    def targets(packed, offset):
        expert = packed[:2] // cap
        position = packed[:2] - expert * cap
        slot = (expert // 2) * (2 * cap) + offset + position
        return jnp.where(expert - (expert // 2) * 2 == core, slot, -1)

    target = jnp.concatenate([targets(routes, 0), targets(routes_other, cap)], axis=1)
    first_gate = jnp.concatenate([routes[2], routes_other[2]]).astype(jnp.float32) / 8.0
    slot_grid = jnp.arange(slots, dtype=jnp.int32)[:, None]
    hit_first = slot_grid == target[0][None, :]
    hit_second = slot_grid == target[1][None, :]
    placing = (hit_first | hit_second).astype(jnp.bfloat16)
    weighing = (
        jnp.where(hit_first, first_gate[None, :], 0.0)
        + jnp.where(hit_second, 1.0 - first_gate[None, :], 0.0)
    ).astype(jnp.bfloat16)


    hidden_rows = shared_down.shape[0]
    groups = shared_up.shape[1] // (2 * hidden_rows)
    nodes = lax.axis_size("z") * lax.axis_size("ylo")
    few = hidden_rows // nodes
    half = groups * hidden_rows
    unit = jnp.arange(2 * half, dtype=jnp.int32)
    inner = lax.rem(unit, half)
    side = jnp.where(unit < half, core, 1 - core)
    picked = (lax.rem(inner // few, groups) * 2 + side) * hidden_rows
    picked = picked + (inner // (groups * few)) * few + lax.rem(inner, few)
    picking = (unit[:, None] == picked[None, :]).astype(jnp.bfloat16)
    by_core = dot(shared_up, picking).astype(jnp.bfloat16)
    up_keep, up_got = by_core[:, :half], swap(by_core[:, half:])
    up_chip = jnp.where(
        core == 0,
        jnp.concatenate([up_keep, up_got], axis=0),
        jnp.concatenate([up_got, up_keep], axis=0),
    )
    shared_in = lax.all_gather(up_chip, LOCAL, axis=0, tiled=True)
    payload = dot(placing, chip_tokens).astype(jnp.bfloat16)
    payload, chip_grads, shared_down = together(payload, chip_grads, shared_down)
    shared_back_out = lax.all_gather(shared_down, LOCAL, axis=0, tiled=True)
    shared_back_out = shared_back_out.reshape(groups, nodes, few, width)
    shared_back_out = shared_back_out.transpose(1, 0, 2, 3).reshape(half, width)
    arrived = exchange(payload)
    upstream = exchange(dot(weighing, chip_grads).astype(jnp.bfloat16))

    shared_pre = dot(chip_tokens, shared_in)
    shared_hidden = gelu_value(shared_pre).astype(jnp.bfloat16)
    term_out = contract_rows(shared_hidden, chip_grads).astype(jnp.bfloat16)
    upward = up_weight[0]
    downward = down_weight[0]
    preact = dot(arrived, upward)
    hidden = gelu_value(preact).astype(jnp.bfloat16)
    produced = dot(hidden, downward).astype(jnp.bfloat16)
    back = jnp.concatenate([produced, term_out], axis=1)
    back, upstream, shared_pre = together(back, upstream, shared_pre)
    returned = exchange(back)

    hidden_grad = contract_cols(upstream, downward)
    slopes = (hidden_grad * gelu_slope(preact)).astype(jnp.bfloat16)
    inward = contract_cols(slopes, upward).astype(jnp.bfloat16)
    shared_back = contract_cols(chip_grads, shared_back_out)
    shared_slopes = (shared_back * gelu_slope(shared_pre)).astype(jnp.bfloat16)
    term_in = contract_rows(chip_tokens, shared_slopes).astype(jnp.bfloat16)
    slab = width // (groups * nodes)
    term_in = term_in.reshape(groups, nodes, slab // few, few, half).transpose(1, 0, 3, 2, 4)
    landed = exchange(jnp.concatenate([inward, term_in.reshape(half, width)], axis=1))

    def total(parts):
        parts = parts.reshape(chips, few, width).astype(jnp.float32)
        return parts.sum(axis=0).astype(jnp.bfloat16)

    def parts_of(routing, rows_back, shared_part):
        near = contract_rows(routing[:, :rows], rows_back) + shared_part[:rows]
        far = contract_rows(routing[:, rows:], rows_back) + shared_part[rows:]
        return near, far.astype(jnp.bfloat16)

    def whole(near, far):
        return (near + swap(far).astype(jnp.float32)).astype(jnp.bfloat16)

    out_near, out_far = parts_of(weighing, returned[:, :width], dot(shared_hidden, shared_back_out))
    shared_grad = contract_cols(shared_slopes, shared_in)
    total_out = total(returned[:, width:])
    out_near, out_far, shared_grad, total_out, slopes = together(
        out_near, out_far, shared_grad, total_out, slopes
    )
    grad_upper = contract_rows(arrived, slopes).astype(jnp.bfloat16)
    grad_lower = contract_rows(hidden, upstream).astype(jnp.bfloat16)

    grad_near, grad_far = parts_of(placing, landed[:, :width], shared_grad)
    totals = jnp.concatenate([total_out, total(landed[:, width:])], axis=1)
    layer_out = whole(out_near, out_far)
    grad_tokens = whole(grad_near, grad_far)
    totals = lax.all_gather(totals, NODE, axis=0, tiled=True)
    sum_out = totals[:, :width].astype(jnp.float32)
    sum_in = totals[:, width:].reshape(nodes, few, slab // few, half).swapaxes(1, 2)
    sum_in = sum_in.reshape(2, -1, half)
    in_keep = lax.dynamic_index_in_dim(sum_in, core, 0, keepdims=False)
    in_got = swap(lax.dynamic_index_in_dim(sum_in, 1 - core, 0, keepdims=False))
    sum_in = contract_cols(jnp.concatenate([in_keep, in_got], axis=1), picking)
    return (layer_out, grad_tokens, grad_upper[None], grad_lower[None], sum_in, sum_out)


def solution(mesh):
    node, local = mesh.shape["node"], mesh.shape["local"]
    fine = Mesh(mesh.devices.reshape(node // 2, 2, local // 4, 2, 2), AXES)
    every = AXES
    shared = ("x", "yhi", "core")
    return jax.shard_map(
        body,
        mesh=fine,
        in_specs=(
            P(every, None),
            P(every, None),
            P(every),
            P(every, None),
            P(every, None, None),
            P(every, None, None),
            P(shared, None),
            P(shared, None),
        ),
        out_specs=(
            P(every, None),
            P(every, None),
            P(every, None, None),
            P(every, None, None),
            P(shared, None),
            P(shared, None),
        ),
        check_vma=False,
    )
```

profile of v0, /device:TPU:1, one launch (start us, length us, event | category | flops | bytes accessed | tf_op | source)
XLA Modules:
  0.0 297.4 jit_solution(24580010296657216)
XLA Ops:
  14.7 2.0 convolution_convert_fusion.3
  16.8 11.5 %all-to-all-start = ((bf16[64,8,2048]{2,1,0:T(8,128)(2,1)}), bf16[64,8,2048]{2,1,0:T(8,128)(2,1)}, u32[]{:S(2)}, u32[]{:S(2)}) async-start(bf16[64,8,2048]{2,1,0:T(8,128)(2,1)} %bitcast.102), calls=%async_computation | async-start | bytes 4194304 | tf_op jit(solution)/shard_map/all_to_all | solution.py:50
  29.0 2.0 fusion.16
  31.1 30.8 %all-to-all-done = bf16[64,8,2048]{2,1,0:T(8,128)(2,1)} async-done(((bf16[64,8,2048]{2,1,0:T(8,128)(2,1)}), bf16[64,8,2048]{2,1,0:T(8,128)(2,1)}, u32[]{:S(2)}, u32[]{:S(2)}) %all-to-all-start) | async-done | bytes 2097184 | tf_op jit(solution)/shard_map/all_to_all | solution.py:50
  61.9 5.8 %all-to-all-start.1 = ((bf16[64,8,2048]{2,1,0:T(8,128)(2,1)}), bf16[64,8,2048]{2,1,0:T(8,128)(2,1)}, u32[]{:S(2)}, u32[]{:S(2)}) async-start(bf16[64,8,2048]{2,1,0:T(8,128)(2,1)} %fusion.16), calls=%async_computation.1 | async-start | bytes 4194304 | tf_op jit(solution)/shard_map/all_to_all | solution.py:50
  67.8 5.4 %fusion.6 = f32[512,1024]{1,0:T(8,128)S(1)} fusion(bf16[1,2048,1024]{2,1,0:T(8,128)(2,1)} %param.12, bf16[64,8,2048]{2,1,0:T(8,128)(2,1)} %all-to-all-done), kind=kOutput, calls=%fused_computation.8 | convolution fusion | flops 2147483648 | bytes 8388608 | tf_op jit(solution)/shard_map/dot_general | solution.py:26
  74.5 3.7 %fusion.13 = bf16[512,2048]{1,0:T(8,128)(2,1)} fusion(bf16[1,1024,2048]{2,1,0:T(8,128)(2,1)S(1)} %copy-done.11, f32[512,1024]{1,0:T(8,128)S(1)} %fusion.6), kind=kOutput, calls=%fused_computation.17 | convolution fusion | flops 2151153664 | bytes 8388608 | tf_op jit(solution)/shard_map/dot_general | solution.py:26
  78.2 3.5 %all-gather.3.cloned.1.call-done = bf16[2048,512]{1,0:T(8,128)(2,1)} async-done(((bf16[256,512]{1,0:T(8,128)(2,1)}), bf16[2048,512]{1,0:T(8,128)(2,1)}) %all-gather.3.cloned.1.call-update) | async-done | bytes 2097168 | tf_op jit(solution)/shard_map/all_gather | solution.py:113
  81.7 2.3 fusion.75
  85.6 2.5 pad_maximum_fusion
  88.1 11.7 %all-to-all-done.1 = bf16[64,8,2048]{2,1,0:T(8,128)(2,1)} async-done(((bf16[64,8,2048]{2,1,0:T(8,128)(2,1)}), bf16[64,8,2048]{2,1,0:T(8,128)(2,1)}, u32[]{:S(2)}, u32[]{:S(2)}) %all-to-all-start.1) | async-done | bytes 2097184 | tf_op jit(solution)/shard_map/all_to_all | solution.py:50
  99.7 5.8 %all-to-all-start.2 = ((bf16[64,8,4096]{2,1,0:T(8,128)(2,1)}), bf16[64,8,4096]{2,1,0:T(8,128)(2,1)}, u32[]{:S(2)}, u32[]{:S(2)}) async-start(bf16[64,8,4096]{2,1,0:T(8,128)(2,1)} %bitcast.99), calls=%async_computation.2 | async-start | bytes 8388608 | tf_op jit(solution)/shard_map/all_to_all | solution.py:50
  105.6 6.4 %fusion.26 = bf16[512,1024]{1,0:T(8,128)(2,1)S(1)} fusion(f32[512,1024]{1,0:T(8,128)} %copy-done.13, bf16[512,2048]{1,0:T(8,128)(2,1)} %bitcast.17, bf16[1,1024,2048]{2,1,0:T(8,128)(2,1)} %param.13), kind=kOutput, calls=%fused_computation.34 | convolution fusion | flops 2152726528 | bytes 9437184 | tf_op jit(solution)/shard_map/dot_general | solution.py:36
  113.1 3.8 %fusion.17 = bf16[64,8,2048]{2,1,0:T(8,128)(2,1)} fusion(bf16[512,1024]{1,0:T(8,128)(2,1)S(1)} %fusion.26, bf16[1,2048,1024]{2,1,0:T(8,128)(2,1)S(1)} %copy-done.12), kind=kOutput, calls=%fused_computation.23 | convolution fusion | flops 2148532224 | bytes 7340032 | tf_op jit(solution)/shard_map/dot_general | solution.py:36
  116.9 58.4 %all-gather.5.cloned.1.call-done = bf16[512,2048]{1,0:T(8,128)(2,1)} async-done(((bf16[64,2048]{1,0:T(8,128)(2,1)}), bf16[512,2048]{1,0:T(8,128)(2,1)}) %all-gather.5.cloned.1.call-update) | async-done | bytes 2097168 | tf_op jit(solution)/shard_map/all_gather | solution.py:116
  175.3 1.7 copy.18
  181.5 2.5 pad_maximum_fusion.1
  184.0 9.4 %all-to-all-start.3 = ((bf16[64,8,4096]{2,1,0:T(8,128)(2,1)}), bf16[64,8,4096]{2,1,0:T(8,128)(2,1)}, u32[]{:S(2)}, u32[]{:S(2)}) async-start(bf16[64,8,4096]{2,1,0:T(8,128)(2,1)} %pad_maximum_fusion.1), calls=%async_computation.3 | async-start | bytes 8388608 | tf_op jit(solution)/shard_map/all_to_all | solution.py:50
  193.7 6.2 %convert_bitcast_fusion = bf16[1,1024,2048]{2,1,0:T(8,128)(2,1)} fusion(bf16[512,2048]{1,0:T(8,128)(2,1)} %bitcast.17, f32[512,1024]{1,0:T(8,128)S(1)} %copy-done.14), kind=kOutput, calls=%fused_computation.10 | convolution fusion | flops 2152202240 | bytes 8388608 | tf_op jit(solution)/shard_map/dot_general | solution.py:30
  202.2 1.9 fusion.28
  204.1 2.9 fusion.20
  207.0 2.1 convolution_add_fusion.3
  209.1 2.6 collective-permute-start.4
  211.8 6.0 %convert_bitcast_fusion.1 = bf16[1,2048,1024]{2,1,0:T(8,128)(2,1)} fusion(bf16[512,1024]{1,0:T(8,128)(2,1)S(1)} %copy-done.16, bf16[64,8,2048]{2,1,0:T(8,128)(2,1)} %all-to-all-done), kind=kOutput, calls=%fused_computation.11 | convolution fusion | flops 2149580800 | bytes 7340032 | tf_op jit(solution)/shard_map/dot_general | solution.py:30
  217.8 30.1 %all-to-all-done.3 = bf16[64,8,4096]{2,1,0:T(8,128)(2,1)} async-done(((bf16[64,8,4096]{2,1,0:T(8,128)(2,1)}), bf16[64,8,4096]{2,1,0:T(8,128)(2,1)}, u32[]{:S(2)}, u32[]{:S(2)}) %all-to-all-start.3) | async-done | bytes 4194336 | tf_op jit(solution)/shard_map/all_to_all | solution.py:50
  247.8 1.9 fusion.27
  249.7 24.4 %all_gather.11 = bf16[64,4096]{1,0:T(8,128)(2,1)S(1)} all-gather(bf16[8,4096]{1,0:T(8,128)(2,1)S(1)} %pad_maximum_fusion.3), channel_id=1, replica_groups=mesh['z'=4,'ylo'=2,'x'=4,'yhi'=2,'core'=2] {'z','ylo'}, dimensions={0}, use_global_device_ids=true | all-gather | bytes 589824 | tf_op jit(solution)/shard_map/all_gather | solution.py:169
  275.0 6.7 %collective-permute-start.6 = (bf16[128,512]{1,0:T(8,128)(2,1)S(1)}, bf16[128,512]{1,0:T(8,128)(2,1)S(1)}, u32[]{:S(2)}, u32[]{:S(2)}) collective-permute-start(bf16[128,512]{1,0:T(8,128)(2,1)S(1)} %get-tuple-element.33), channel_id=1, source_target_pairs={{0,1},{1,0},{2,3},{3,2},{4,5},{5,4},{6,7},{7,6},{8,9},{9,8},{10,11... | collective-permute-start | bytes 393224 | tf_op jit(solution)/shard_map/ppermute | solution.py:46
  281.7 2.1 fusion.21
  283.9 1.8 fusion.8
  285.7 2.0 add_convert_fusion.1
  287.7 2.9 add_convert_fusion
  (79 shorter events, 20.1 us)
Async XLA Ops:
  7.2 1.6 copy-start
  7.2 5.7 %copy-start.7 = (bf16[128,2048]{1,0:T(8,128)(2,1)S(1)}, bf16[128,2048]{1,0:T(8,128)(2,1)}, u32[]{:S(2)}) copy-start(bf16[128,2048]{1,0:T(8,128)(2,1)} %param.8) | copy-start | bytes 1572868
  7.2 3.3 %copy-start.9 = (s32[128,2]{0,1:T(2,128)S(1)}, s32[128,2]{0,1:T(2,128)}, u32[]{:S(2)}) copy-start(s32[128,2]{0,1:T(2,128)} %param.9) | copy-start | bytes 3076
  7.2 5.1 %copy-start.10 = (s32[128]{0:T(128)S(1)}, s32[128]{0:T(128)}, u32[]{:S(2)}) copy-start(s32[128]{0:T(128)} %param.10) | copy-start | bytes 1540
  7.2 5.5 %copy-start.8 = (bf16[128,2048]{1,0:T(8,128)(2,1)S(1)}, bf16[128,2048]{1,0:T(8,128)(2,1)}, u32[]{:S(2)}) copy-start(bf16[128,2048]{1,0:T(8,128)(2,1)} %param.11) | copy-start | bytes 1572868
  7.2 74.5 %all-gather.3.cloned.1.call-start = ((), (), s32[]{:S(2)}) async-start(), calls=%async_computation.4 | async-start | bytes 2359296 | tf_op jit(solution)/shard_map/all_gather | solution.py:113
  7.3 6.3 %collective-permute-start.1 = (bf16[128,2048]{1,0:T(8,128)(2,1)}, bf16[128,2048]{1,0:T(8,128)(2,1)S(1)}, u32[]{:S(2)}, u32[]{:S(2)}) collective-permute-start(bf16[128,2048]{1,0:T(8,128)(2,1)} %param.8), channel_id=1, source_target_pairs={{0,1},{1,0},{2,3},{3,2},{4,5},{5,4},{6,7},{7,6},{8,9},{9,8},{10,11... | collective-permute-start | bytes 1572872 | tf_op jit(solution)/shard_map/ppermute | solution.py:46
  9.7 1.8 collective-permute-start.3
  12.3 1.3 collective-permute-start
  12.7 1.9 collective-permute-start.2
  16.8 45.1 %all-to-all-start = ((bf16[64,8,2048]{2,1,0:T(8,128)(2,1)}), bf16[64,8,2048]{2,1,0:T(8,128)(2,1)}, u32[]{:S(2)}, u32[]{:S(2)}) async-start(bf16[64,8,2048]{2,1,0:T(8,128)(2,1)} %bitcast.102), calls=%async_computation | async-start | bytes 4194304 | tf_op jit(solution)/shard_map/all_to_all | solution.py:50
  28.3 147.0 %all-gather.5.cloned.1.call-start = ((), (), s32[]{:S(2)}) async-start(), calls=%async_computation.5 | async-start | bytes 2359296 | tf_op jit(solution)/shard_map/all_gather | solution.py:116
  61.9 37.8 %all-to-all-start.1 = ((bf16[64,8,2048]{2,1,0:T(8,128)(2,1)}), bf16[64,8,2048]{2,1,0:T(8,128)(2,1)}, u32[]{:S(2)}, u32[]{:S(2)}) async-start(bf16[64,8,2048]{2,1,0:T(8,128)(2,1)} %fusion.16), calls=%async_computation.1 | async-start | bytes 4194304 | tf_op jit(solution)/shard_map/all_to_all | solution.py:50
  67.8 6.7 %copy-start.11 = (bf16[1,1024,2048]{2,1,0:T(8,128)(2,1)S(1)}, bf16[1,1024,2048]{2,1,0:T(8,128)(2,1)}, u32[]{:S(2)}) copy-start(bf16[1,1024,2048]{2,1,0:T(8,128)(2,1)} %param.13) | copy-start | bytes 12582916
  73.2 1.3 copy-start.13
  84.0 1.6 copy-start.6
  99.7 84.3 %all-to-all-start.2 = ((bf16[64,8,4096]{2,1,0:T(8,128)(2,1)}), bf16[64,8,4096]{2,1,0:T(8,128)(2,1)}, u32[]{:S(2)}, u32[]{:S(2)}) async-start(bf16[64,8,4096]{2,1,0:T(8,128)(2,1)} %bitcast.99), calls=%async_computation.2 | async-start | bytes 8388608 | tf_op jit(solution)/shard_map/all_to_all | solution.py:50
  105.6 7.5 %copy-start.12 = (bf16[1,2048,1024]{2,1,0:T(8,128)(2,1)S(1)}, bf16[1,2048,1024]{2,1,0:T(8,128)(2,1)}, u32[]{:S(2)}) copy-start(bf16[1,2048,1024]{2,1,0:T(8,128)(2,1)} %param.12) | copy-start | bytes 12582916
  112.0 1.0 copy-start.15
  177.0 1.3 copy-start.2
  179.9 1.6 copy-start.5
  184.0 9.7 %copy-start.14 = (f32[512,1024]{1,0:T(8,128)S(1)}, f32[512,1024]{1,0:T(8,128)}, u32[]{:S(2)}) copy-start(f32[512,1024]{1,0:T(8,128)} %copy-done.13) | copy-start | bytes 6291460
  184.0 63.8 %all-to-all-start.3 = ((bf16[64,8,4096]{2,1,0:T(8,128)(2,1)}), bf16[64,8,4096]{2,1,0:T(8,128)(2,1)}, u32[]{:S(2)}, u32[]{:S(2)}) async-start(bf16[64,8,4096]{2,1,0:T(8,128)(2,1)} %pad_maximum_fusion.1), calls=%async_computation.3 | async-start | bytes 8388608 | tf_op jit(solution)/shard_map/all_to_all | solution.py:50
  193.7 6.2 %copy-start.4 = (bf16[2048,512]{1,0:T(8,128)(2,1)S(1)}, bf16[2048,512]{1,0:T(8,128)(2,1)}, u32[]{:S(2)}) copy-start(bf16[2048,512]{1,0:T(8,128)(2,1)} %all-gather.3.cloned.1.call-done) | copy-start | bytes 6291460
  199.9 1.6 copy-start.3
  207.0 4.8 %copy-start.16 = (bf16[512,1024]{1,0:T(8,128)(2,1)S(1)}, bf16[512,1024]{1,0:T(8,128)(2,1)}, u32[]{:S(2)}) copy-start(bf16[512,1024]{1,0:T(8,128)(2,1)} %copy-done.15) | copy-start | bytes 3145732
  209.1 76.5 %collective-permute-start.4 = (bf16[128,2048]{1,0:T(8,128)(2,1)}, bf16[128,2048]{1,0:T(8,128)(2,1)}, u32[]{:S(2)}, u32[]{:S(2)}) collective-permute-start(bf16[128,2048]{1,0:T(8,128)(2,1)} %fusion.20), channel_id=1, source_target_pairs={{0,1},{1,0},{2,3},{3,2},{4,5},{5,4},{6,7},{7,6},{8,9},{9,8},{10,11... | collective-permute-start | bytes 1572872 | tf_op jit(solution)/shard_map/ppermute | solution.py:46
  275.0 8.9 %collective-permute-start.6 = (bf16[128,512]{1,0:T(8,128)(2,1)S(1)}, bf16[128,512]{1,0:T(8,128)(2,1)S(1)}, u32[]{:S(2)}, u32[]{:S(2)}) collective-permute-start(bf16[128,512]{1,0:T(8,128)(2,1)S(1)} %get-tuple-element.33), channel_id=1, source_target_pairs={{0,1},{1,0},{2,3},{3,2},{4,5},{5,4},{6,7},{7,6},{8,9},{9,8},{10,11... | collective-permute-start | bytes 393224 | tf_op jit(solution)/shard_map/ppermute | solution.py:46
  283.8 3.8 %collective-permute-start.5 = (bf16[128,2048]{1,0:T(8,128)(2,1)S(1)}, bf16[128,2048]{1,0:T(8,128)(2,1)S(1)}, u32[]{:S(2)}, u32[]{:S(2)}) collective-permute-start(bf16[128,2048]{1,0:T(8,128)(2,1)S(1)} %fusion.21), channel_id=1, source_target_pairs={{0,1},{1,0},{2,3},{3,2},{4,5},{5,4},{6,7},{7,6},{8,9},{9,8},{10,11... | collective-permute-start | bytes 1572872 | tf_op jit(solution)/shard_map/ppermute | solution.py:46
  285.7 4.9 %copy-start.1 = (bf16[128,1024]{1,0:T(8,128)(2,1)S(1)}, bf16[128,1024]{1,0:T(8,128)(2,1)}, u32[]{:S(2)}) copy-start(bf16[128,1024]{1,0:T(8,128)(2,1)} %param.14) | copy-start | bytes 786436
Sparse Core Ops, SparseCore 0:
  12.4 69.2 all-gather.2
  84.0 91.1 all-gather.4
where the time goes:
time: 298 us; the launch traced here: 297 us
  waiting for transfers between devices  138 us (46%)
  matrix products  54.1 us (18%)
  starting transfers between devices  45 us (15%)
  blocking collectives  24.4 us (8%)
  between operations  14.4 us (5%)
  other arithmetic  13 us (4%)
  local copies, waits for them, and re-layouts  8.83 us (3%)
    all_to_all x4, waiting for transfers between devices, exchange(): lax.all_to_all(values, CHIPS, split_axis=0, concat_axis=0, tiled=True)  72.6 us
    all_gather x1, waiting for transfers between devices, body(): shared_back_out = lax.all_gather(shared_down, LOCAL, axis=0, tiled=True)  58.4 us
    all_to_all x4, starting transfers between devices, exchange(): lax.all_to_all(values, CHIPS, split_axis=0, concat_axis=0, tiled=True)  32.6 us
    all_gather x1, blocking collectives, body(): totals = lax.all_gather(totals, NODE, axis=0, tiled=True)  24.4 us
    dot_general x8, matrix products, contract_rows(): lax.dot_general(left, right, (((0,), (0,)), ((), ())), preferred_element_...  23.6 us
    dot_general x7, matrix products, dot(): return jnp.dot(left, right, preferred_element_type=jnp.float32)  17 us
    dot_general x5, matrix products, contract_cols(): lax.dot_general(left, right, (((1,), (1,)), ((), ())), preferred_element_...  13.5 us
    ppermute x7, starting transfers between devices, swap(): return lax.ppermute(values, 'core', [(0, 1), (1, 0)])  12.4 us
  transfers between devices with their start and end apart: 13, of which 8 were waited for; matrix products, arithmetic and copies ran while one was open for 22% of the time, Pallas kernels for 0%

commit v1 on v0

--- a/solution.py
+++ b/solution.py
@@ -8,8 +8,6 @@
 
 AXES = ("z", "ylo", "x", "yhi", "core")
 CHIPS = ("z", "ylo", "x", "yhi")
-LOCAL = ("x", "yhi")
-NODE = ("z", "ylo")
 
 
 def gelu_value(values):
@@ -44,6 +42,19 @@
 
 def swap(values):
     return lax.ppermute(values, "core", [(0, 1), (1, 0)])
+
+
+def gather(values, axis):
+    count = lax.axis_size(axis)
+    here = lax.axis_index(axis)
+    out = jnp.zeros((count,) + values.shape, values.dtype)
+    zeros = (0,) * values.ndim
+    for step in range(count):
+        piece = values
+        if step:
+            piece = lax.ppermute(values, axis, [((i + step) % count, i) for i in range(count)])
+        out = lax.dynamic_update_slice(out, piece[None], (lax.rem(here + step, count),) + zeros)
+    return out
 
 
 def exchange(values):
@@ -110,14 +121,23 @@
         jnp.concatenate([up_keep, up_got], axis=0),
         jnp.concatenate([up_got, up_keep], axis=0),
     )
-    shared_in = lax.all_gather(up_chip, LOCAL, axis=0, tiled=True)
-    payload = dot(placing, chip_tokens).astype(jnp.bfloat16)
-    payload, chip_grads, shared_down = together(payload, chip_grads, shared_down)
-    shared_back_out = lax.all_gather(shared_down, LOCAL, axis=0, tiled=True)
-    shared_back_out = shared_back_out.reshape(groups, nodes, few, width)
-    shared_back_out = shared_back_out.transpose(1, 0, 2, 3).reshape(half, width)
-    arrived = exchange(payload)
-    upstream = exchange(dot(weighing, chip_grads).astype(jnp.bfloat16))
+    node = lax.axis_index("z") * lax.axis_size("ylo") + lax.axis_index("ylo")
+    slab = width // (groups * nodes)
+    up_slab = lax.dynamic_slice_in_dim(up_chip, node * slab, slab, 0)
+    up_slab = up_slab.reshape(slab // few, few, half).swapaxes(0, 1).reshape(few, width)
+    down_slab = lax.dynamic_slice_in_dim(shared_down, node * few, few, 0)
+
+    def beside(routed, slab_rows):
+        copies = jnp.broadcast_to(slab_rows[None], (chips, few, width)).reshape(chips * few, width)
+        return jnp.concatenate([routed, copies], axis=1)
+
+    payload = beside(dot(placing, chip_tokens).astype(jnp.bfloat16), up_slab)
+    payload, chip_grads, down_slab = together(payload, chip_grads, down_slab)
+    arrived_both = exchange(payload)
+    upstream_both = exchange(beside(dot(weighing, chip_grads).astype(jnp.bfloat16), down_slab))
+    arrived = arrived_both[:, :width]
+    shared_in = arrived_both[:, width:].reshape(nodes, groups, few, slab // few, half)
+    shared_in = shared_in.transpose(1, 0, 3, 2, 4).reshape(width, half)
 
     shared_pre = dot(chip_tokens, shared_in)
     shared_hidden = gelu_value(shared_pre).astype(jnp.bfloat16)
@@ -128,8 +148,9 @@
     hidden = gelu_value(preact).astype(jnp.bfloat16)
     produced = dot(hidden, downward).astype(jnp.bfloat16)
     back = jnp.concatenate([produced, term_out], axis=1)
-    back, upstream, shared_pre = together(back, upstream, shared_pre)
+    back, upstream_both, shared_pre = together(back, upstream_both, shared_pre)
     returned = exchange(back)
+    upstream, shared_back_out = upstream_both[:, :width], upstream_both[:, width:]
 
     hidden_grad = contract_cols(upstream, downward)
     slopes = (hidden_grad * gelu_slope(preact)).astype(jnp.bfloat16)
@@ -137,7 +158,6 @@
     shared_back = contract_cols(chip_grads, shared_back_out)
     shared_slopes = (shared_back * gelu_slope(shared_pre)).astype(jnp.bfloat16)
     term_in = contract_rows(chip_tokens, shared_slopes).astype(jnp.bfloat16)
-    slab = width // (groups * nodes)
     term_in = term_in.reshape(groups, nodes, slab // few, few, half).transpose(1, 0, 3, 2, 4)
     landed = exchange(jnp.concatenate([inward, term_in.reshape(half, width)], axis=1))
 
@@ -162,11 +182,12 @@
     grad_upper = contract_rows(arrived, slopes).astype(jnp.bfloat16)
     grad_lower = contract_rows(hidden, upstream).astype(jnp.bfloat16)
 
+    landed, grad_upper, grad_lower = together(landed, grad_upper, grad_lower)
     grad_near, grad_far = parts_of(placing, landed[:, :width], shared_grad)
     totals = jnp.concatenate([total_out, total(landed[:, width:])], axis=1)
     layer_out = whole(out_near, out_far)
     grad_tokens = whole(grad_near, grad_far)
-    totals = lax.all_gather(totals, NODE, axis=0, tiled=True)
+    totals = gather(gather(totals, "ylo"), "z").reshape(nodes * few, 2 * width)
     sum_out = totals[:, :width].astype(jnp.float32)
     sum_in = totals[:, width:].reshape(nodes, few, slab // few, half).swapaxes(1, 2)
     sum_in = sum_in.reshape(2, -1, half)

time: 298 us -> 289 us (0.970)
  waiting for transfers between devices: 138 us -> 164 us
  blocking collectives: 24.4 us -> 0 us
  between operations: 14.4 us -> 1.21 us
  local copies, waits for them, and re-layouts: 8.83 us -> 18.2 us
  starting transfers between devices: 45 us -> 39.5 us
  matrix products: 54.1 us -> 48.8 us
  other arithmetic: 13 us -> 16.2 us
    all_to_all x4, waiting for transfers between devices: 72.6 us -> 152 us  [exchange(): lax.all_to_all(values, CHIPS, split_axis=0, concat_axis=0, tiled=True)]
    all_gather x2 -> x0, waiting for transfers between devices: 61.9 us -> none  [the longest x1 58.4 us: body(): shared_back_out = lax.all_gather(shared_down, LOCAL, axis=0, tiled=True)]
    all_gather x1 -> x0, blocking collectives: 24.4 us -> none  [body(): totals = lax.all_gather(totals, NODE, axis=0, tiled=True)]
    ppermute x0 -> x4, waiting for transfers between devices: none -> 11.7 us  [gather(): lax.ppermute(values, axis, [((i + step) % count, i) for i in range(count)])]
    ppermute x7, starting transfers between devices: 12.4 us -> 5.2 us  [swap(): return lax.ppermute(values, 'core', [(0, 1), (1, 0)])]
    dot_general x7, matrix products: 17 us -> 11.9 us  [dot(): return jnp.dot(left, right, preferred_element_type=jnp.float32)]
    concatenate x0 -> x2, other arithmetic: none -> 5.03 us  [beside(): return jnp.concatenate([routed, copies], axis=1)]
    reshape x0 -> x2, local copies, waits for them, and re-layouts: none -> 4.79 us  [the longest x1 4.55 us: body(): arrived_both[:, width:].reshape(nodes, groups, few, slab // few, half)]
  transfers between devices with their start and end apart: 13 -> 15, of which waited for: 8 -> 10; matrix products, arithmetic and copies ran while one was open for 22% -> 25% of each run, Pallas kernels for 0% -> 0%
where the time goes in v1:
time: 289 us; the launch traced here: 288 us
  waiting for transfers between devices  164 us (57%)
  matrix products  48.8 us (17%)
  starting transfers between devices  39.5 us (14%)
  local copies, waits for them, and re-layouts  18.2 us (6%)
  other arithmetic  16.2 us (6%)
    all_to_all x4, waiting for transfers between devices, exchange(): lax.all_to_all(values, CHIPS, split_axis=0, concat_axis=0, tiled=True)  152 us
    all_to_all x4, starting transfers between devices, exchange(): lax.all_to_all(values, CHIPS, split_axis=0, concat_axis=0, tiled=True)  32.7 us
    dot_general x8, matrix products, contract_rows(): lax.dot_general(left, right, (((0,), (0,)), ((), ())), preferred_element_...  23.5 us
    dot_general x5, matrix products, contract_cols(): lax.dot_general(left, right, (((1,), (1,)), ((), ())), preferred_element_...  13.4 us
    dot_general x7, matrix products, dot(): return jnp.dot(left, right, preferred_element_type=jnp.float32)  11.9 us
    ppermute x4, waiting for transfers between devices, gather(): lax.ppermute(values, axis, [((i + step) % count, i) for i in range(count)])  11.7 us
    unnamed x39, local copies, waits for them, and re-layouts  5.91 us
  transfers between devices with their start and end apart: 15, of which 10 were waited for; matrix products, arithmetic and copies ran while one was open for 25% of the time, Pallas kernels for 0%

profile of v1, /device:TPU:1, one launch (start us, length us, event | category | flops | bytes accessed | tf_op | source)
XLA Modules:
  0.0 288.1 jit_solution(18090803465835055635)
XLA Ops:
  7.6 2.5 pad_maximum_fusion
  10.2 11.5 %all-to-all-start = ((bf16[64,8,4096]{2,1,0:T(8,128)(2,1)}), bf16[64,8,4096]{2,1,0:T(8,128)(2,1)}, u32[]{:S(2)}, u32[]{:S(2)}) async-start(bf16[64,8,4096]{2,1,0:T(8,128)(2,1)} %bitcast.105), calls=%async_computation | async-start | bytes 8388608 | tf_op jit(solution)/shard_map/all_to_all | solution.py:61
  22.7 2.5 pad_maximum_fusion.2
  25.2 50.4 %all-to-all-done = bf16[64,8,4096]{2,1,0:T(8,128)(2,1)} async-done(((bf16[64,8,4096]{2,1,0:T(8,128)(2,1)}), bf16[64,8,4096]{2,1,0:T(8,128)(2,1)}, u32[]{:S(2)}, u32[]{:S(2)}) %all-to-all-start) | async-done | bytes 4194336 | tf_op jit(solution)/shard_map/all_to_all | solution.py:61
  75.6 6.7 %all-to-all-start.1 = ((bf16[64,8,4096]{2,1,0:T(8,128)(2,1)}), bf16[64,8,4096]{2,1,0:T(8,128)(2,1)}, u32[]{:S(2)}, u32[]{:S(2)}) async-start(bf16[64,8,4096]{2,1,0:T(8,128)(2,1)} %pad_maximum_fusion.2), calls=%async_computation.1 | async-start | bytes 8388608 | tf_op jit(solution)/shard_map/all_to_all | solution.py:61
  82.3 3.2 %slice.128 = bf16[512,2048]{1,0:T(8,128)(2,1)} slice(bf16[512,4096]{1,0:T(8,128)(2,1)} %bitcast.17), slice={[0:512], [2048:4096]} | slice | bytes 4194304 | tf_op jit(solution)/shard_map/slice | solution.py:139
  85.4 4.5 %reshape.136 = bf16[8,8,8,4,512]{4,3,2,1,0:T(4,128)(2,1)} reshape(bf16[512,2048]{1,0:T(8,128)(2,1)} %slice.128) | data formatting | bytes 4194304 | tf_op jit(solution)/shard_map/reshape | solution.py:139
  90.0 2.2 copy.18
  95.1 4.1 %fusion.6 = f32[512,1024]{1,0:T(8,128)S(1)} fusion(bf16[1,2048,1024]{2,1,0:T(8,128)(2,1)S(1)} %copy-done.12, bf16[512,4096]{1,0:T(8,128)(2,1)} %bitcast.17), kind=kOutput, calls=%fused_computation.10 | convolution fusion | flops 2147483648 | bytes 8388608 | tf_op jit(solution)/shard_map/dot_general | solution.py:24
  100.6 2.4 fusion.13
  103.0 2.5 pad_maximum_fusion.1
  105.5 31.2 %all-to-all-done.1 = bf16[64,8,4096]{2,1,0:T(8,128)(2,1)} async-done(((bf16[64,8,4096]{2,1,0:T(8,128)(2,1)}), bf16[64,8,4096]{2,1,0:T(8,128)(2,1)}, u32[]{:S(2)}, u32[]{:S(2)}) %all-to-all-start.1) | async-done | bytes 4194336 | tf_op jit(solution)/shard_map/all_to_all | solution.py:61
  136.7 7.0 %all-to-all-start.2 = ((bf16[64,8,4096]{2,1,0:T(8,128)(2,1)}), bf16[64,8,4096]{2,1,0:T(8,128)(2,1)}, u32[]{:S(2)}, u32[]{:S(2)}) async-start(bf16[64,8,4096]{2,1,0:T(8,128)(2,1)} %bitcast.106), calls=%async_computation.2 | async-start | bytes 8388608 | tf_op jit(solution)/shard_map/all_to_all | solution.py:61
  143.7 2.4 fusion.49
  149.2 4.7 %fusion.26 = bf16[512,1024]{1,0:T(8,128)(2,1)S(1)} fusion(f32[512,1024]{1,0:T(8,128)S(1)} %copy-done.15, bf16[1,1024,2048]{2,1,0:T(8,128)(2,1)S(1)} %copy-done.11, bf16[512,4096]{1,0:T(8,128)(2,1)} %bitcast.23), kind=kOutput, calls=%fused_computation.36 | convolution fusion | flops 2152726528 | bytes 9437184 | tf_op jit(solution)/shard_map/dot_general | solution.py:34
  153.9 2.4 fusion.17
  156.3 2.4 pad_maximum_fusion.3
  158.7 39.4 %all-to-all-done.2 = bf16[64,8,4096]{2,1,0:T(8,128)(2,1)} async-done(((bf16[64,8,4096]{2,1,0:T(8,128)(2,1)}), bf16[64,8,4096]{2,1,0:T(8,128)(2,1)}, u32[]{:S(2)}, u32[]{:S(2)}) %all-to-all-start.2) | async-done | bytes 4194336 | tf_op jit(solution)/shard_map/all_to_all | solution.py:61
  198.2 7.6 %all-to-all-start.3 = ((bf16[64,8,4096]{2,1,0:T(8,128)(2,1)}), bf16[64,8,4096]{2,1,0:T(8,128)(2,1)}, u32[]{:S(2)}, u32[]{:S(2)}) async-start(bf16[64,8,4096]{2,1,0:T(8,128)(2,1)} %pad_maximum_fusion.3), calls=%async_computation.3 | async-start | bytes 8388608 | tf_op jit(solution)/shard_map/all_to_all | solution.py:61
  206.1 2.1 fusion.90
  208.2 2.5 fusion.40
  210.7 6.0 %convolution_convert_fusion = bf16[1024,2048]{1,0:T(8,128)(2,1)} fusion(bf16[512,4096]{1,0:T(8,128)(2,1)} %bitcast.23, f32[512,1024]{1,0:T(8,128)S(1)} %copy-done.16), kind=kOutput, calls=%fused_computation.15 | convolution fusion | flops 2152202240 | bytes 8388608 | tf_op jit(solution)/shard_map/dot_general | solution.py:28
  218.6 2.9 fusion.20
  221.5 2.1 convolution_add_fusion.3
  223.7 6.0 %convolution_convert_fusion.1 = bf16[2048,1024]{1,0:T(8,128)(2,1)} fusion(bf16[512,1024]{1,0:T(8,128)(2,1)S(1)} %copy-done.18, bf16[512,4096]{1,0:T(8,128)(2,1)} %bitcast.17), kind=kOutput, calls=%fused_computation.16 | convolution fusion | flops 2149580800 | bytes 7340032 | tf_op jit(solution)/shard_map/dot_general | solution.py:28
  229.7 30.5 %all-to-all-done.3 = bf16[64,8,4096]{2,1,0:T(8,128)(2,1)} async-done(((bf16[64,8,4096]{2,1,0:T(8,128)(2,1)}), bf16[64,8,4096]{2,1,0:T(8,128)(2,1)}, u32[]{:S(2)}, u32[]{:S(2)}) %all-to-all-start.3) | async-done | bytes 4194336 | tf_op jit(solution)/shard_map/all_to_all | solution.py:61
  262.1 2.1 fusion.21
  264.2 2.3 collective-permute-start.5
  266.5 3.6 %collective-permute-done.6 = bf16[8,4096]{1,0:T(8,128)(2,1)S(1)} collective-permute-done((bf16[8,4096]{1,0:T(8,128)(2,1)S(1)}, bf16[8,4096]{1,0:T(8,128)(2,1)S(1)}, u32[]{:S(2)}, u32[]{:S(2)}) %collective-permute-start.6) | collective-permute-done | bytes 65568 | tf_op jit(solution)/shard_map/ppermute | solution.py:55
  271.8 2.6 collective-permute-done.7
  276.0 3.9 %collective-permute-done.9 = bf16[2,8,4096]{2,1,0:T(8,128)(2,1)S(1)} collective-permute-done((bf16[2,8,4096]{2,1,0:T(8,128)(2,1)S(1)}, bf16[2,8,4096]{2,1,0:T(8,128)(2,1)S(1)}, u32[]{:S(2)}, u32[]{:S(2)}) %collective-permute-start.9) | collective-permute-done | bytes 131104 | tf_op jit(solution)/shard_map/ppermute | solution.py:55
  284.3 2.9 %add_convert_fusion = bf16[128,2048]{1,0:T(8,128)(2,1)} fusion(bf16[128,2048]{1,0:T(8,128)(2,1)S(1)} %collective-permute-done.5, f32[256,2048]{1,0:T(8,128)S(1)} %copy-done.4, bf16[512,4096]{1,0:T(8,128)(2,1)} %bitcast.31, pred[512,256]{1,0:T(32,128)(4,1)S(1)} %fusion.59), kind=kOutput, calls=%fused_computation.61 | convolution fusion | flops 269484032 | bytes 4259840 | tf_op jit(solution)/shard_map/dot_general | solution.py:28
  (99 shorter events, 27.8 us)
Async XLA Ops:
  0.6 3.9 %copy-start.5 = (bf16[128,2048]{1,0:T(8,128)(2,1)S(1)}, bf16[128,2048]{1,0:T(8,128)(2,1)}, u32[]{:S(2)}) copy-start(bf16[128,2048]{1,0:T(8,128)(2,1)} %param.8) | copy-start | bytes 1572868
  0.7 3.9 %copy-start.8 = (s32[128,2]{0,1:T(2,128)S(1)}, s32[128,2]{0,1:T(2,128)}, u32[]{:S(2)}) copy-start(s32[128,2]{0,1:T(2,128)} %param.9) | copy-start | bytes 3076
  0.7 4.0 %copy-start.9 = (s32[128]{0:T(128)S(1)}, s32[128]{0:T(128)}, u32[]{:S(2)}) copy-start(s32[128]{0:T(128)} %param.10) | copy-start | bytes 1540
  0.7 4.6 %copy-start.6 = (bf16[128,2048]{1,0:T(8,128)(2,1)S(1)}, bf16[128,2048]{1,0:T(8,128)(2,1)}, u32[]{:S(2)}) copy-start(bf16[128,2048]{1,0:T(8,128)(2,1)} %param.11) | copy-start | bytes 1572868
  3.1 3.4 %collective-permute-start.2 = (bf16[128,512]{1,0:T(8,128)(2,1)}, bf16[128,512]{1,0:T(8,128)(2,1)S(1)}, u32[]{:S(2)}, u32[]{:S(2)}) collective-permute-start(bf16[128,512]{1,0:T(8,128)(2,1)} %get-tuple-element.41), channel_id=1, source_target_pairs={{0,1},{1,0},{2,3},{3,2},{4,5},{5,4},{6,7},{7,6},{8,9},{9,8},{10,11... | collective-permute-start | bytes 393224 | tf_op jit(solution)/shard_map/ppermute | solution.py:44
  4.5 2.3 collective-permute-start.1
  4.7 1.7 collective-permute-start
  5.3 4.8 %collective-permute-start.3 = (bf16[128,2048]{1,0:T(8,128)(2,1)S(1)}, bf16[128,2048]{1,0:T(8,128)(2,1)S(1)}, u32[]{:S(2)}, u32[]{:S(2)}) collective-permute-start(bf16[128,2048]{1,0:T(8,128)(2,1)S(1)} %copy-done.6), channel_id=1, source_target_pairs={{0,1},{1,0},{2,3},{3,2},{4,5},{5,4},{6,7},{7,6},{8,9},{9,8},{10,11... | collective-permute-start | bytes 1572872 | tf_op jit(solution)/shard_map/ppermute | solution.py:44
  10.2 65.4 %all-to-all-start = ((bf16[64,8,4096]{2,1,0:T(8,128)(2,1)}), bf16[64,8,4096]{2,1,0:T(8,128)(2,1)}, u32[]{:S(2)}, u32[]{:S(2)}) async-start(bf16[64,8,4096]{2,1,0:T(8,128)(2,1)} %bitcast.105), calls=%async_computation | async-start | bytes 8388608 | tf_op jit(solution)/shard_map/all_to_all | solution.py:61
  75.6 61.1 %all-to-all-start.1 = ((bf16[64,8,4096]{2,1,0:T(8,128)(2,1)}), bf16[64,8,4096]{2,1,0:T(8,128)(2,1)}, u32[]{:S(2)}, u32[]{:S(2)}) async-start(bf16[64,8,4096]{2,1,0:T(8,128)(2,1)} %pad_maximum_fusion.2), calls=%async_computation.1 | async-start | bytes 8388608 | tf_op jit(solution)/shard_map/all_to_all | solution.py:61
  92.2 1.5 copy-start.2
  92.2 2.9 %copy-start.12 = (bf16[1,2048,1024]{2,1,0:T(8,128)(2,1)S(1)}, bf16[1,2048,1024]{2,1,0:T(8,128)(2,1)}, u32[]{:S(2)}) copy-start(bf16[1,2048,1024]{2,1,0:T(8,128)(2,1)} %param.12) | copy-start | bytes 12582916
  95.1 5.5 %copy-start.10 = (bf16[1,1024,2048]{2,1,0:T(8,128)(2,1)S(1)}, bf16[1,1024,2048]{2,1,0:T(8,128)(2,1)}, u32[]{:S(2)}) copy-start(bf16[1,1024,2048]{2,1,0:T(8,128)(2,1)} %param.13) | copy-start | bytes 12582916
  136.7 61.5 %all-to-all-start.2 = ((bf16[64,8,4096]{2,1,0:T(8,128)(2,1)}), bf16[64,8,4096]{2,1,0:T(8,128)(2,1)}, u32[]{:S(2)}, u32[]{:S(2)}) async-start(bf16[64,8,4096]{2,1,0:T(8,128)(2,1)} %bitcast.106), calls=%async_computation.2 | async-start | bytes 8388608 | tf_op jit(solution)/shard_map/all_to_all | solution.py:61
  146.1 1.6 copy-start.15
  146.9 2.3 copy-start.11
  149.2 4.7 %copy-start.13 = (bf16[1,2048,1024]{2,1,0:T(8,128)(2,1)S(1)}, bf16[1,2048,1024]{2,1,0:T(8,128)(2,1)}, u32[]{:S(2)}) copy-start(bf16[1,2048,1024]{2,1,0:T(8,128)(2,1)} %param.12) | copy-start | bytes 12582916
  153.9 2.4 copy-start.17
  158.7 47.3 %copy-start.3 = (bf16[8,8,4,8,512]{4,3,2,1,0:T(8,128)(2,1)S(1)}, bf16[8,8,4,8,512]{4,3,2,1,0:T(8,128)(2,1)}, u32[]{:S(2)}) copy-start(bf16[8,8,4,8,512]{4,3,2,1,0:T(8,128)(2,1)} %copy-done.2) | copy-start | bytes 6291460
  198.2 62.0 %all-to-all-start.3 = ((bf16[64,8,4096]{2,1,0:T(8,128)(2,1)}), bf16[64,8,4096]{2,1,0:T(8,128)(2,1)}, u32[]{:S(2)}, u32[]{:S(2)}) async-start(bf16[64,8,4096]{2,1,0:T(8,128)(2,1)} %pad_maximum_fusion.3), calls=%async_computation.3 | async-start | bytes 8388608 | tf_op jit(solution)/shard_map/all_to_all | solution.py:61
  208.2 2.5 copy-start.16
  221.5 2.2 copy-start.18
  229.7 32.5 %copy-start.4 = (f32[256,2048]{1,0:T(8,128)S(1)}, f32[256,2048]{1,0:T(8,128)}, u32[]{:S(2)}) copy-start(f32[256,2048]{1,0:T(8,128)} %fusion.90) | copy-start | bytes 6291460
  264.2 17.3 %copy-start.7 = (bf16[128,2048]{1,0:T(8,128)(2,1)S(1)}, bf16[128,2048]{1,0:T(8,128)(2,1)}, u32[]{:S(2)}) copy-start(bf16[128,2048]{1,0:T(8,128)(2,1)} %fusion.20) | copy-start | bytes 1572868
  264.2 20.1 %collective-permute-start.5 = (bf16[128,2048]{1,0:T(8,128)(2,1)S(1)}, bf16[128,2048]{1,0:T(8,128)(2,1)S(1)}, u32[]{:S(2)}, u32[]{:S(2)}) collective-permute-start(bf16[128,2048]{1,0:T(8,128)(2,1)S(1)} %fusion.21), channel_id=1, source_target_pairs={{0,1},{1,0},{2,3},{3,2},{4,5},{5,4},{6,7},{7,6},{8,9},{9,8},{10,11... | collective-permute-start | bytes 1572872 | tf_op jit(solution)/shard_map/ppermute | solution.py:44
  266.5 3.7 %collective-permute-start.6 = (bf16[8,4096]{1,0:T(8,128)(2,1)S(1)}, bf16[8,4096]{1,0:T(8,128)(2,1)S(1)}, u32[]{:S(2)}, u32[]{:S(2)}) collective-permute-start(bf16[8,4096]{1,0:T(8,128)(2,1)S(1)} %pad_maximum_fusion.5), channel_id=1, source_target_pairs={{16,0},{0,16},{17,1},{1,17},{18,2},{2,18},{19,3},{3,19},{20,4},{4,... | collective-permute-start | bytes 196616 | tf_op jit(solution)/shard_map/ppermute | solution.py:55
  270.2 4.2 %collective-permute-start.7 = (bf16[2,8,4096]{2,1,0:T(8,128)(2,1)S(1)}, bf16[2,8,4096]{2,1,0:T(8,128)(2,1)S(1)}, u32[]{:S(2)}, u32[]{:S(2)}) collective-permute-start(bf16[2,8,4096]{2,1,0:T(8,128)(2,1)S(1)} %bitcast_dynamic-update-slice_fusion.4), channel_id=1, source_target_pairs={{32,0},{64,32},{96,64},{0,96},{33,1},{65,33},{97,65},{1,97},{34,2}... | collective-permute-start | bytes 393224 | tf_op jit(solution)/shard_map/ppermute | solution.py:55
  270.3 5.7 %collective-permute-start.8 = (bf16[2,8,4096]{2,1,0:T(8,128)(2,1)S(1)}, bf16[2,8,4096]{2,1,0:T(8,128)(2,1)S(1)}, u32[]{:S(2)}, u32[]{:S(2)}) collective-permute-start(bf16[2,8,4096]{2,1,0:T(8,128)(2,1)S(1)} %bitcast_dynamic-update-slice_fusion.4), channel_id=1, source_target_pairs={{64,0},{96,32},{0,64},{32,96},{65,1},{97,33},{1,65},{33,97},{66,2}... | collective-permute-start | bytes 393224 | tf_op jit(solution)/shard_map/ppermute | solution.py:55
  270.7 9.2 %collective-permute-start.9 = (bf16[2,8,4096]{2,1,0:T(8,128)(2,1)S(1)}, bf16[2,8,4096]{2,1,0:T(8,128)(2,1)S(1)}, u32[]{:S(2)}, u32[]{:S(2)}) collective-permute-start(bf16[2,8,4096]{2,1,0:T(8,128)(2,1)S(1)} %bitcast_dynamic-update-slice_fusion.4), channel_id=1, source_target_pairs={{96,0},{0,32},{32,64},{64,96},{97,1},{1,33},{33,65},{65,97},{98,2}... | collective-permute-start | bytes 393224 | tf_op jit(solution)/shard_map/ppermute | solution.py:55
  280.8 1.7 collective-permute-start.10
  281.5 5.7 %collective-permute-start.4 = (bf16[128,2048]{1,0:T(8,128)(2,1)S(1)}, bf16[128,2048]{1,0:T(8,128)(2,1)S(1)}, u32[]{:S(2)}, u32[]{:S(2)}) collective-permute-start(bf16[128,2048]{1,0:T(8,128)(2,1)S(1)} %copy-done.7), channel_id=1, source_target_pairs={{0,1},{1,0},{2,3},{3,2},{4,5},{5,4},{6,7},{7,6},{8,9},{9,8},{10,11... | collective-permute-start | bytes 1572872 | tf_op jit(solution)/shard_map/ppermute | solution.py:44
  284.3 3.9 %copy-start.1 = (bf16[128,1024]{1,0:T(8,128)(2,1)S(1)}, bf16[128,1024]{1,0:T(8,128)(2,1)}, u32[]{:S(2)}) copy-start(bf16[128,1024]{1,0:T(8,128)(2,1)} %param.14) | copy-start | bytes 786436
  (2 other events, 2.3 us)

commit v2 on v1

--- a/solution.py
+++ b/solution.py
@@ -127,43 +127,39 @@
     up_slab = up_slab.reshape(slab // few, few, half).swapaxes(0, 1).reshape(few, width)
     down_slab = lax.dynamic_slice_in_dim(shared_down, node * few, few, 0)
 
-    def beside(routed, slab_rows):
-        copies = jnp.broadcast_to(slab_rows[None], (chips, few, width)).reshape(chips * few, width)
-        return jnp.concatenate([routed, copies], axis=1)
-
-    payload = beside(dot(placing, chip_tokens).astype(jnp.bfloat16), up_slab)
-    payload, chip_grads, down_slab = together(payload, chip_grads, down_slab)
+    def copies(slab_rows):
+        return jnp.broadcast_to(slab_rows[None], (chips, few, width)).reshape(chips * few, width)
+
+    payload = jnp.concatenate(
+        [dot(placing, chip_tokens).astype(jnp.bfloat16), copies(up_slab), copies(down_slab)], axis=1
+    )
+    payload, chip_grads = together(payload, chip_grads)
     arrived_both = exchange(payload)
-    upstream_both = exchange(beside(dot(weighing, chip_grads).astype(jnp.bfloat16), down_slab))
+    upstream = exchange(dot(weighing, chip_grads).astype(jnp.bfloat16))
     arrived = arrived_both[:, :width]
-    shared_in = arrived_both[:, width:].reshape(nodes, groups, few, slab // few, half)
+    shared_back_out = arrived_both[:, 2 * width :]
+    shared_in = arrived_both[:, width : 2 * width].reshape(nodes, groups, few, slab // few, half)
     shared_in = shared_in.transpose(1, 0, 3, 2, 4).reshape(width, half)
 
     shared_pre = dot(chip_tokens, shared_in)
     shared_hidden = gelu_value(shared_pre).astype(jnp.bfloat16)
+    shared_back = contract_cols(chip_grads, shared_back_out)
+    shared_slopes = (shared_back * gelu_slope(shared_pre)).astype(jnp.bfloat16)
     term_out = contract_rows(shared_hidden, chip_grads).astype(jnp.bfloat16)
+    term_in = contract_rows(chip_tokens, shared_slopes).astype(jnp.bfloat16)
+    term_in = term_in.reshape(groups, nodes, slab // few, few, half).transpose(1, 0, 3, 2, 4)
+
     upward = up_weight[0]
     downward = down_weight[0]
     preact = dot(arrived, upward)
     hidden = gelu_value(preact).astype(jnp.bfloat16)
     produced = dot(hidden, downward).astype(jnp.bfloat16)
-    back = jnp.concatenate([produced, term_out], axis=1)
-    back, upstream_both, shared_pre = together(back, upstream_both, shared_pre)
+    back = jnp.concatenate([produced, term_out, term_in.reshape(half, width)], axis=1)
+    back, upstream = together(back, upstream)
     returned = exchange(back)
-    upstream, shared_back_out = upstream_both[:, :width], upstream_both[:, width:]
-
     hidden_grad = contract_cols(upstream, downward)
     slopes = (hidden_grad * gelu_slope(preact)).astype(jnp.bfloat16)
     inward = contract_cols(slopes, upward).astype(jnp.bfloat16)
-    shared_back = contract_cols(chip_grads, shared_back_out)
-    shared_slopes = (shared_back * gelu_slope(shared_pre)).astype(jnp.bfloat16)
-    term_in = contract_rows(chip_tokens, shared_slopes).astype(jnp.bfloat16)
-    term_in = term_in.reshape(groups, nodes, slab // few, few, half).transpose(1, 0, 3, 2, 4)
-    landed = exchange(jnp.concatenate([inward, term_in.reshape(half, width)], axis=1))
-
-    def total(parts):
-        parts = parts.reshape(chips, few, width).astype(jnp.float32)
-        return parts.sum(axis=0).astype(jnp.bfloat16)
 
     def parts_of(routing, rows_back, shared_part):
         near = contract_rows(routing[:, :rows], rows_back) + shared_part[:rows]
@@ -173,21 +169,22 @@
     def whole(near, far):
         return (near + swap(far).astype(jnp.float32)).astype(jnp.bfloat16)
 
+    totals = returned[:, width:].reshape(chips, few, 2 * width).astype(jnp.float32)
+    totals = gather(totals.sum(axis=0).astype(jnp.bfloat16), "ylo")
+    inward, totals = together(inward, totals)
+    landed = exchange(inward)
+    totals = gather(totals, "z").reshape(nodes * few, 2 * width)
+    totals, returned, slopes = together(totals, returned, slopes)
+
     out_near, out_far = parts_of(weighing, returned[:, :width], dot(shared_hidden, shared_back_out))
     shared_grad = contract_cols(shared_slopes, shared_in)
-    total_out = total(returned[:, width:])
-    out_near, out_far, shared_grad, total_out, slopes = together(
-        out_near, out_far, shared_grad, total_out, slopes
-    )
+    out_near, out_far, shared_grad, slopes = together(out_near, out_far, shared_grad, slopes)
     grad_upper = contract_rows(arrived, slopes).astype(jnp.bfloat16)
     grad_lower = contract_rows(hidden, upstream).astype(jnp.bfloat16)
-
     landed, grad_upper, grad_lower = together(landed, grad_upper, grad_lower)
-    grad_near, grad_far = parts_of(placing, landed[:, :width], shared_grad)
-    totals = jnp.concatenate([total_out, total(landed[:, width:])], axis=1)
+    grad_near, grad_far = parts_of(placing, landed, shared_grad)
     layer_out = whole(out_near, out_far)
     grad_tokens = whole(grad_near, grad_far)
-    totals = gather(gather(totals, "ylo"), "z").reshape(nodes * few, 2 * width)
     sum_out = totals[:, :width].astype(jnp.float32)
     sum_in = totals[:, width:].reshape(nodes, few, slab // few, half).swapaxes(1, 2)
     sum_in = sum_in.reshape(2, -1, half)

time: 289 us -> 298 us (1.031)
  starting transfers between devices: 39.5 us -> 52.1 us
  waiting for transfers between devices: 164 us -> 152 us
  other arithmetic: 16.2 us -> 21.4 us
  matrix products: 48.8 us -> 52.8 us
    ppermute x4, waiting for transfers between devices: 11.7 us -> 3.07 us  [gather(): lax.ppermute(values, axis, [((i + step) % count, i) for i in range(count)])]
    all_to_all x4, starting transfers between devices: 32.7 us -> 38.7 us  [exchange(): lax.all_to_all(values, CHIPS, split_axis=0, concat_axis=0, tiled=True)]
    ppermute x7, starting transfers between devices: 5.2 us -> 10.6 us  [swap(): return lax.ppermute(values, 'core', [(0, 1), (1, 0)])]
    all_to_all x4, waiting for transfers between devices: 152 us -> 148 us  [exchange(): lax.all_to_all(values, CHIPS, split_axis=0, concat_axis=0, tiled=True)]
    concatenate x5 -> x2, other arithmetic: 9.97 us -> 12.8 us  [the longest x1 6.4 us: body(): jnp.concatenate([produced, term_out, term_in.reshape(half, width)], axis=1)]
  transfers between devices with their start and end apart: 15 -> 15, of which waited for: 10 -> 4; matrix products, arithmetic and copies ran while one was open for 25% -> 27% of each run, Pallas kernels for 0% -> 0%
where the time goes in v2:
time: 298 us; the launch traced here: 297 us
  waiting for transfers between devices  152 us (51%)
  matrix products  52.8 us (18%)
  starting transfers between devices  52.1 us (17%)
  other arithmetic  21.4 us (7%)
  local copies, waits for them, and re-layouts  17.5 us (6%)
    all_to_all x4, waiting for transfers between devices, exchange(): lax.all_to_all(values, CHIPS, split_axis=0, concat_axis=0, tiled=True)  148 us
    all_to_all x4, starting transfers between devices, exchange(): lax.all_to_all(values, CHIPS, split_axis=0, concat_axis=0, tiled=True)  38.7 us
    dot_general x8, matrix products, contract_rows(): lax.dot_general(left, right, (((0,), (0,)), ((), ())), preferred_element_...  22.3 us
    dot_general x5, matrix products, contract_cols(): lax.dot_general(left, right, (((1,), (1,)), ((), ())), preferred_element_...  16 us
    dot_general x7, matrix products, dot(): return jnp.dot(left, right, preferred_element_type=jnp.float32)  14.5 us
    ppermute x7, starting transfers between devices, swap(): return lax.ppermute(values, 'core', [(0, 1), (1, 0)])  10.6 us
    concatenate x1, other arithmetic, body(): jnp.concatenate([produced, term_out, term_in.reshape(half, width)], axis=1)  6.4 us
    concatenate x1, other arithmetic, body(): jnp.concatenate([dot(placing, chip_tokens).astype(jnp.bfloat16), copies(u...  6.4 us
  transfers between devices with their start and end apart: 15, of which 4 were waited for; matrix products, arithmetic and copies ran while one was open for 27% of the time, Pallas kernels for 0%

profile of v2, /device:TPU:1, one launch (start us, length us, event | category | flops | bytes accessed | tf_op | source)
XLA Modules:
  0.0 296.6 jit_solution(13130738261330589075)
XLA Ops:
  9.1 6.4 %pad_maximum_fusion = bf16[512,6144]{1,0:T(8,128)(2,1)} fusion(bf16[512,2048]{1,0:T(8,128)(2,1)S(1)} %get-tuple-element.56, bf16[512,2048]{1,0:T(8,128)(2,1)S(1)} %get-tuple-element.57, bf16[512,2048]{1,0:T(8,128)(2,1)S(1)} %convolution_convert_fusion.5), kind=kLoop, calls=%fused_computation | loop fusion | flops 18874368 | bytes 12582912 | tf_op jit(solution)/shard_map/concatenate | solution.py:133
  16.6 11.5 %all-to-all-start = ((bf16[64,8,6144]{2,1,0:T(8,128)(2,1)}), bf16[64,8,6144]{2,1,0:T(8,128)(2,1)}, u32[]{:S(2)}, u32[]{:S(2)}) async-start(bf16[64,8,6144]{2,1,0:T(8,128)(2,1)} %bitcast.104), calls=%async_computation | async-start | bytes 12582912 | tf_op jit(solution)/shard_map/all_to_all | solution.py:61
  28.1 2.0 fusion.17
  30.2 83.2 %all-to-all-done = bf16[64,8,6144]{2,1,0:T(8,128)(2,1)} async-done(((bf16[64,8,6144]{2,1,0:T(8,128)(2,1)}), bf16[64,8,6144]{2,1,0:T(8,128)(2,1)}, u32[]{:S(2)}, u32[]{:S(2)}) %all-to-all-start) | async-done | bytes 6291488 | tf_op jit(solution)/shard_map/all_to_all | solution.py:61
  113.4 5.8 %all-to-all-start.1 = ((bf16[64,8,2048]{2,1,0:T(8,128)(2,1)}), bf16[64,8,2048]{2,1,0:T(8,128)(2,1)}, u32[]{:S(2)}, u32[]{:S(2)}) async-start(bf16[64,8,2048]{2,1,0:T(8,128)(2,1)} %fusion.17), calls=%async_computation.1 | async-start | bytes 4194304 | tf_op jit(solution)/shard_map/all_to_all | solution.py:61
  119.1 2.3 fusion.29
  121.5 3.2 %slice.116 = bf16[512,2048]{1,0:T(8,128)(2,1)} slice(bf16[512,6144]{1,0:T(8,128)(2,1)} %bitcast.18), slice={[0:512], [2048:4096]} | slice | bytes 4194304 | tf_op jit(solution)/shard_map/slice | solution.py:141
  124.6 4.5 %reshape.132 = bf16[8,8,8,4,512]{4,3,2,1,0:T(4,128)(2,1)} reshape(bf16[512,2048]{1,0:T(8,128)(2,1)} %slice.116) | data formatting | bytes 4194304 | tf_op jit(solution)/shard_map/reshape | solution.py:141
  129.1 2.2 copy.18
  134.6 1.9 copy-done.14
  136.5 4.1 %fusion.7 = f32[512,1024]{1,0:T(8,128)S(1)} fusion(bf16[1,2048,1024]{2,1,0:T(8,128)(2,1)S(1)} %copy-done.14, bf16[512,6144]{1,0:T(8,128)(2,1)} %bitcast.18), kind=kOutput, calls=%fused_computation.10 | convolution fusion | flops 2147483648 | bytes 8388608 | tf_op jit(solution)/shard_map/dot_general | solution.py:24
  140.6 2.3 fusion.14
  143.0 6.4 %pad_maximum_fusion.1 = bf16[512,6144]{1,0:T(8,128)(2,1)} fusion(bf16[512,2048]{1,0:T(8,128)(2,1)S(1)} %bitcast.111, bf16[512,2048]{1,0:T(8,128)(2,1)S(1)} %convolution_convert_fusion.4, bf16[512,2048]{1,0:T(8,128)(2,1)S(1)} %fusion.14), kind=kLoop, calls=%fused_computation.1 | loop fusion | flops 18874368 | bytes 12582912 | tf_op jit(solution)/shard_map/concatenate | solution.py:157
  149.4 10.0 %all-to-all-start.2 = ((bf16[64,8,6144]{2,1,0:T(8,128)(2,1)}), bf16[64,8,6144]{2,1,0:T(8,128)(2,1)}, u32[]{:S(2)}, u32[]{:S(2)}) async-start(bf16[64,8,6144]{2,1,0:T(8,128)(2,1)} %bitcast.103), calls=%async_computation.2 | async-start | bytes 12582912 | tf_op jit(solution)/shard_map/all_to_all | solution.py:61
  159.7 3.8 %fusion.27 = f32[256,2048]{1,0:T(8,128)} fusion(bf16[512,6144]{1,0:T(8,128)(2,1)} %bitcast.18, f32[256,512]{1,0:T(8,128)S(1)} %fusion.77), kind=kOutput, calls=%fused_computation.40 | convolution fusion | flops 537526272 | bytes 4718592 | tf_op jit(solution)/shard_map/dot_general | solution.py:24
  163.4 2.1 fusion.73
  165.6 6.2 %convolution_convert_fusion = bf16[1024,2048]{1,0:T(8,128)(2,1)} fusion(bf16[512,2048]{1,0:T(8,128)(2,1)} %bitcast.27, f32[512,1024]{1,0:T(8,128)S(1)} %copy-done.17), kind=kOutput, calls=%fused_computation.15 | convolution fusion | flops 2152202240 | bytes 8388608 | tf_op jit(solution)/shard_map/dot_general | solution.py:28
  171.8 5.0 %fusion.24 = bf16[512,1024]{1,0:T(8,128)(2,1)S(1)} fusion(f32[512,1024]{1,0:T(8,128)S(1)} %copy-done.17, bf16[512,2048]{1,0:T(8,128)(2,1)} %bitcast.27, bf16[1,1024,2048]{2,1,0:T(8,128)(2,1)S(1)} %copy-done.13), kind=kOutput, calls=%fused_computation.35 | convolution fusion | flops 2152726528 | bytes 9437184 | tf_op jit(solution)/shard_map/dot_general | solution.py:34
  177.7 3.8 %fusion.11 = bf16[512,2048]{1,0:T(8,128)(2,1)} fusion(bf16[512,1024]{1,0:T(8,128)(2,1)S(1)} %fusion.24, bf16[1,2048,1024]{2,1,0:T(8,128)(2,1)S(1)} %copy-done.15), kind=kOutput, calls=%fused_computation.18 | convolution fusion | flops 2148532224 | bytes 7340032 | tf_op jit(solution)/shard_map/dot_general | solution.py:34
  181.5 56.0 %all-to-all-done.2 = bf16[64,8,6144]{2,1,0:T(8,128)(2,1)} async-done(((bf16[64,8,6144]{2,1,0:T(8,128)(2,1)}), bf16[64,8,6144]{2,1,0:T(8,128)(2,1)}, u32[]{:S(2)}, u32[]{:S(2)}) %all-to-all-start.2) | async-done | bytes 6291488 | tf_op jit(solution)/shard_map/all_to_all | solution.py:61
  237.5 2.8 fusion
  240.4 3.1 %collective-permute-done.4 = bf16[8,4096]{1,0:T(8,128)(2,1)S(1)} collective-permute-done((bf16[8,4096]{1,0:T(8,128)(2,1)S(1)}, bf16[8,4096]{1,0:T(8,128)(2,1)S(1)}, u32[]{:S(2)}, u32[]{:S(2)}) %collective-permute-start.4) | collective-permute-done | bytes 65568 | tf_op jit(solution)/shard_map/ppermute | solution.py:55
  243.6 2.7 collective-permute-start.6
  246.3 11.5 %all-to-all-start.3 = ((bf16[64,8,2048]{2,1,0:T(8,128)(2,1)}), bf16[64,8,2048]{2,1,0:T(8,128)(2,1)S(1)}, u32[]{:S(2)}, u32[]{:S(2)}) async-start(bf16[64,8,2048]{2,1,0:T(8,128)(2,1)} %bitcast.112), calls=%async_computation.3 | async-start | bytes 4194304 | tf_op jit(solution)/shard_map/all_to_all | solution.py:61
  258.0 3.3 %fusion.18 = bf16[128,2048]{1,0:T(8,128)(2,1)} fusion(bf16[512,6144]{1,0:T(8,128)(2,1)} %bitcast.29, f32[256,2048]{1,0:T(8,128)} %fusion.27, bf16[512,256]{1,0:T(8,128)(2,1)S(1)} %add_convert_fusion.2), kind=kOutput, calls=%fused_computation.29 | convolution fusion | flops 268959744 | bytes 3801088 | tf_op jit(solution)/shard_map/dot_general | solution.py:28
  261.3 2.2 convolution_add_fusion.3
  263.4 3.9 %collective-permute-start.8 = (bf16[128,2048]{1,0:T(8,128)(2,1)}, bf16[128,2048]{1,0:T(8,128)(2,1)}, u32[]{:S(2)}, u32[]{:S(2)}) collective-permute-start(bf16[128,2048]{1,0:T(8,128)(2,1)} %fusion.18), channel_id=1, source_target_pairs={{0,1},{1,0},{2,3},{3,2},{4,5},{5,4},{6,7},{7,6},{8,9},{9,8},{10,11... | collective-permute-start | bytes 1572872 | tf_op jit(solution)/shard_map/ppermute | solution.py:44
  268.9 6.0 %convolution_convert_fusion.1 = bf16[2048,1024]{1,0:T(8,128)(2,1)} fusion(bf16[512,1024]{1,0:T(8,128)(2,1)S(1)} %copy-done.19, bf16[512,6144]{1,0:T(8,128)(2,1)} %bitcast.18), kind=kOutput, calls=%fused_computation.16 | convolution fusion | flops 2149580800 | bytes 7340032 | tf_op jit(solution)/shard_map/dot_general | solution.py:28
  274.9 9.2 %all-to-all-done.3 = bf16[64,8,2048]{2,1,0:T(8,128)(2,1)S(1)} async-done(((bf16[64,8,2048]{2,1,0:T(8,128)(2,1)}), bf16[64,8,2048]{2,1,0:T(8,128)(2,1)S(1)}, u32[]{:S(2)}, u32[]{:S(2)}) %all-to-all-start.3) | async-done | bytes 2097184 | tf_op jit(solution)/shard_map/all_to_all | solution.py:61
  285.9 4.6 %collective-permute-start.9 = (bf16[128,2048]{1,0:T(8,128)(2,1)S(1)}, bf16[128,2048]{1,0:T(8,128)(2,1)S(1)}, u32[]{:S(2)}, u32[]{:S(2)}) collective-permute-start(bf16[128,2048]{1,0:T(8,128)(2,1)S(1)} %fusion.19), channel_id=1, source_target_pairs={{0,1},{1,0},{2,3},{3,2},{4,5},{5,4},{6,7},{7,6},{8,9},{9,8},{10,11... | collective-permute-start | bytes 1572872 | tf_op jit(solution)/shard_map/ppermute | solution.py:44
  290.5 2.8 fusion.9
  293.3 2.0 add_convert_fusion.1
  (96 shorter events, 18.8 us)
Async XLA Ops:
  0.6 4.6 %copy-start = (bf16[128,1024]{1,0:T(8,128)(2,1)S(1)}, bf16[128,1024]{1,0:T(8,128)(2,1)}, u32[]{:S(2)}) copy-start(bf16[128,1024]{1,0:T(8,128)(2,1)} %param.14) | copy-start | bytes 786436
  0.6 5.5 %copy-start.6 = (bf16[128,2048]{1,0:T(8,128)(2,1)S(1)}, bf16[128,2048]{1,0:T(8,128)(2,1)}, u32[]{:S(2)}) copy-start(bf16[128,2048]{1,0:T(8,128)(2,1)} %param.8) | copy-start | bytes 1572868
  0.7 6.0 %copy-start.7 = (bf16[128,2048]{1,0:T(8,128)(2,1)S(1)}, bf16[128,2048]{1,0:T(8,128)(2,1)}, u32[]{:S(2)}) copy-start(bf16[128,2048]{1,0:T(8,128)(2,1)} %param.11) | copy-start | bytes 1572868
  3.8 3.9 %collective-permute-start = (s32[3,128]{1,0:T(4,128)S(1)}, s32[3,128]{1,0:T(4,128)S(1)}, u32[]{:S(2)}, u32[]{:S(2)}) collective-permute-start(s32[3,128]{1,0:T(4,128)S(1)} %pad_add_fusion), channel_id=1, source_target_pairs={{0,1},{1,0},{2,3},{3,2},{4,5},{5,4},{6,7},{7,6},{8,9},{9,8},{10,11... | collective-permute-start | bytes 4616 | tf_op jit(solution)/shard_map/ppermute | solution.py:44
  5.2 3.1 %copy-start.9 = (s32[1024]{0:T(1024)}, s32[1024]{0:T(1024)S(1)}, u32[]{:S(2)}) copy-start(s32[1024]{0:T(1024)S(1)} %fusion.62) | copy-start | bytes 12292
  6.1 1.6 collective-permute-start.2
  6.2 2.1 collective-permute-start.1
  6.7 8.8 %collective-permute-start.3 = (bf16[128,2048]{1,0:T(8,128)(2,1)S(1)}, bf16[128,2048]{1,0:T(8,128)(2,1)}, u32[]{:S(2)}, u32[]{:S(2)}) collective-permute-start(bf16[128,2048]{1,0:T(8,128)(2,1)S(1)} %copy-done.7), channel_id=1, source_target_pairs={{0,1},{1,0},{2,3},{3,2},{4,5},{5,4},{6,7},{7,6},{8,9},{9,8},{10,11... | collective-permute-start | bytes 1572872 | tf_op jit(solution)/shard_map/ppermute | solution.py:44
  16.6 11.5 %copy-start.11 = (s32[128]{0:T(128)S(1)}, s32[128]{0:T(128)}, u32[]{:S(2)}) copy-start(s32[128]{0:T(128)} %param.10) | copy-start | bytes 1540
  16.6 96.7 %all-to-all-start = ((bf16[64,8,6144]{2,1,0:T(8,128)(2,1)}), bf16[64,8,6144]{2,1,0:T(8,128)(2,1)}, u32[]{:S(2)}, u32[]{:S(2)}) async-start(bf16[64,8,6144]{2,1,0:T(8,128)(2,1)} %bitcast.104), calls=%async_computation | async-start | bytes 12582912 | tf_op jit(solution)/shard_map/all_to_all | solution.py:61
  113.4 36.0 %all-to-all-start.1 = ((bf16[64,8,2048]{2,1,0:T(8,128)(2,1)}), bf16[64,8,2048]{2,1,0:T(8,128)(2,1)}, u32[]{:S(2)}, u32[]{:S(2)}) async-start(bf16[64,8,2048]{2,1,0:T(8,128)(2,1)} %fusion.17), calls=%async_computation.1 | async-start | bytes 4194304 | tf_op jit(solution)/shard_map/all_to_all | solution.py:61
  134.3 2.2 copy-start.14
  136.5 4.1 %copy-start.12 = (bf16[1,1024,2048]{2,1,0:T(8,128)(2,1)S(1)}, bf16[1,1024,2048]{2,1,0:T(8,128)(2,1)}, u32[]{:S(2)}) copy-start(bf16[1,1024,2048]{2,1,0:T(8,128)(2,1)} %param.13) | copy-start | bytes 12582916
  140.6 2.4 copy-start.16
  149.4 88.1 %all-to-all-start.2 = ((bf16[64,8,6144]{2,1,0:T(8,128)(2,1)}), bf16[64,8,6144]{2,1,0:T(8,128)(2,1)}, u32[]{:S(2)}, u32[]{:S(2)}) async-start(bf16[64,8,6144]{2,1,0:T(8,128)(2,1)} %bitcast.103), calls=%async_computation.2 | async-start | bytes 12582912 | tf_op jit(solution)/shard_map/all_to_all | solution.py:61
  159.6 3.8 %copy-start.3 = (bf16[8,8,4,8,512]{4,3,2,1,0:T(8,128)(2,1)S(1)}, bf16[8,8,4,8,512]{4,3,2,1,0:T(8,128)(2,1)}, u32[]{:S(2)}) copy-start(bf16[8,8,4,8,512]{4,3,2,1,0:T(8,128)(2,1)} %copy-done.2) | copy-start | bytes 6291460
  165.6 6.2 %copy-start.13 = (bf16[1,1024,2048]{2,1,0:T(8,128)(2,1)S(1)}, bf16[1,1024,2048]{2,1,0:T(8,128)(2,1)}, u32[]{:S(2)}) copy-start(bf16[1,1024,2048]{2,1,0:T(8,128)(2,1)} %param.13) | copy-start | bytes 12582916
  171.8 6.0 %copy-start.15 = (bf16[1,2048,1024]{2,1,0:T(8,128)(2,1)S(1)}, bf16[1,2048,1024]{2,1,0:T(8,128)(2,1)}, u32[]{:S(2)}) copy-start(bf16[1,2048,1024]{2,1,0:T(8,128)(2,1)} %param.12) | copy-start | bytes 12582916
  240.3 3.2 %collective-permute-start.4 = (bf16[8,4096]{1,0:T(8,128)(2,1)S(1)}, bf16[8,4096]{1,0:T(8,128)(2,1)S(1)}, u32[]{:S(2)}, u32[]{:S(2)}) collective-permute-start(bf16[8,4096]{1,0:T(8,128)(2,1)S(1)} %fusion), channel_id=1, source_target_pairs={{16,0},{0,16},{17,1},{1,17},{18,2},{2,18},{19,3},{3,19},{20,4},{4,... | collective-permute-start | bytes 196616 | tf_op jit(solution)/shard_map/ppermute | solution.py:55
  243.5 14.5 %collective-permute-start.7 = (bf16[2,8,4096]{2,1,0:T(8,128)(2,1)S(1)}, bf16[2,8,4096]{2,1,0:T(8,128)(2,1)S(1)}, u32[]{:S(2)}, u32[]{:S(2)}) collective-permute-start(bf16[2,8,4096]{2,1,0:T(8,128)(2,1)S(1)} %bitcast_dynamic-update-slice_fusion.4), channel_id=1, source_target_pairs={{96,0},{0,32},{32,64},{64,96},{97,1},{1,33},{33,65},{65,97},{98,2}... | collective-permute-start | bytes 393224 | tf_op jit(solution)/shard_map/ppermute | solution.py:55
  243.6 14.3 %collective-permute-start.6 = (bf16[2,8,4096]{2,1,0:T(8,128)(2,1)S(1)}, bf16[2,8,4096]{2,1,0:T(8,128)(2,1)S(1)}, u32[]{:S(2)}, u32[]{:S(2)}) collective-permute-start(bf16[2,8,4096]{2,1,0:T(8,128)(2,1)S(1)} %bitcast_dynamic-update-slice_fusion.4), channel_id=1, source_target_pairs={{64,0},{96,32},{0,64},{32,96},{65,1},{97,33},{1,65},{33,97},{66,2}... | collective-permute-start | bytes 393224 | tf_op jit(solution)/shard_map/ppermute | solution.py:55
  246.3 11.6 %collective-permute-start.5 = (bf16[2,8,4096]{2,1,0:T(8,128)(2,1)S(1)}, bf16[2,8,4096]{2,1,0:T(8,128)(2,1)S(1)}, u32[]{:S(2)}, u32[]{:S(2)}) collective-permute-start(bf16[2,8,4096]{2,1,0:T(8,128)(2,1)S(1)} %bitcast_dynamic-update-slice_fusion.4), channel_id=1, source_target_pairs={{32,0},{64,32},{96,64},{0,96},{33,1},{65,33},{97,65},{1,97},{34,2}... | collective-permute-start | bytes 393224 | tf_op jit(solution)/shard_map/ppermute | solution.py:55
  246.3 37.9 %all-to-all-start.3 = ((bf16[64,8,2048]{2,1,0:T(8,128)(2,1)}), bf16[64,8,2048]{2,1,0:T(8,128)(2,1)S(1)}, u32[]{:S(2)}, u32[]{:S(2)}) async-start(bf16[64,8,2048]{2,1,0:T(8,128)(2,1)} %bitcast.112), calls=%async_computation.3 | async-start | bytes 4194304 | tf_op jit(solution)/shard_map/all_to_all | solution.py:61
  258.0 3.3 %copy-start.5 = (f32[256,2048]{1,0:T(8,128)S(1)}, f32[256,2048]{1,0:T(8,128)}, u32[]{:S(2)}) copy-start(f32[256,2048]{1,0:T(8,128)} %fusion.27) | copy-start | bytes 6291460
  261.3 7.6 %copy-start.19 = (bf16[512,1024]{1,0:T(8,128)(2,1)S(1)}, bf16[512,1024]{1,0:T(8,128)(2,1)}, u32[]{:S(2)}) copy-start(bf16[512,1024]{1,0:T(8,128)(2,1)} %copy-done.18) | copy-start | bytes 3145732
  263.4 29.9 %collective-permute-start.8 = (bf16[128,2048]{1,0:T(8,128)(2,1)}, bf16[128,2048]{1,0:T(8,128)(2,1)}, u32[]{:S(2)}, u32[]{:S(2)}) collective-permute-start(bf16[128,2048]{1,0:T(8,128)(2,1)} %fusion.18), channel_id=1, source_target_pairs={{0,1},{1,0},{2,3},{3,2},{4,5},{5,4},{6,7},{7,6},{8,9},{9,8},{10,11... | collective-permute-start | bytes 1572872 | tf_op jit(solution)/shard_map/ppermute | solution.py:44
  268.9 21.6 %collective-permute-start.10 = (bf16[128,512]{1,0:T(8,128)(2,1)}, bf16[128,512]{1,0:T(8,128)(2,1)}, u32[]{:S(2)}, u32[]{:S(2)}) collective-permute-start(bf16[128,512]{1,0:T(8,128)(2,1)} %get-tuple-element.43), channel_id=1, source_target_pairs={{0,1},{1,0},{2,3},{3,2},{4,5},{5,4},{6,7},{7,6},{8,9},{9,8},{10,11... | collective-permute-start | bytes 393224 | tf_op jit(solution)/shard_map/ppermute | solution.py:44
  274.9 15.6 %copy-start.8 = (bf16[128,512]{1,0:T(8,128)(2,1)S(1)}, bf16[128,512]{1,0:T(8,128)(2,1)}, u32[]{:S(2)}) copy-start(bf16[128,512]{1,0:T(8,128)(2,1)} %get-tuple-element.42) | copy-start | bytes 393220
  274.9 15.6 %copy-start.10 = (s32[1024]{0:T(1024)S(1)}, s32[1024]{0:T(1024)}, u32[]{:S(2)}) copy-start(s32[1024]{0:T(1024)} %copy-done.9) | copy-start | bytes 12292
  285.9 9.4 %collective-permute-start.9 = (bf16[128,2048]{1,0:T(8,128)(2,1)S(1)}, bf16[128,2048]{1,0:T(8,128)(2,1)S(1)}, u32[]{:S(2)}, u32[]{:S(2)}) collective-permute-start(bf16[128,2048]{1,0:T(8,128)(2,1)S(1)} %fusion.19), channel_id=1, source_target_pairs={{0,1},{1,0},{2,3},{3,2},{4,5},{5,4},{6,7},{7,6},{8,9},{9,8},{10,11... | collective-permute-start | bytes 1572872 | tf_op jit(solution)/shard_map/ppermute | solution.py:44
  290.5 4.8 %copy-start.4 = (f32[256,2048]{1,0:T(8,128)S(1)}, f32[256,2048]{1,0:T(8,128)}, u32[]{:S(2)}) copy-start(f32[256,2048]{1,0:T(8,128)} %fusion.73) | copy-start | bytes 6291460
  293.3 3.3 %copy-start.1 = (bf16[128,1024]{1,0:T(8,128)(2,1)S(1)}, bf16[128,1024]{1,0:T(8,128)(2,1)}, u32[]{:S(2)}) copy-start(bf16[128,1024]{1,0:T(8,128)(2,1)} %param.14) | copy-start | bytes 786436
  (3 other events, 4.5 us)
